TPU v7x, 32 devices: a whole 2x2x4 slice. The times are simulated.
32 devices in a mesh: rep: 4 (over x, core), fsdp: 8 (over z, y).
Axes of the slice: x: 2, y: 2, z: 4, core: 2. Of those that a mesh axis runs over, the one named last changes fastest.
Arguments:
- decoder_input: bfloat16 [8, 1024, 768], P('fsdp', 'rep'), may hold values from -6 to 6
- memory: bfloat16 [8, 3072, 768], P('fsdp', 'rep'), may hold values from -6 to 6
- memory_lengths: int32 [8], P('fsdp'), may hold values from 2305 to 3072, as said below
- distance_bucket: int32 [1024], replicated, may hold values from 0 to 31, as said below
- cotangent: float32 [8, 1024, 768], P('fsdp', 'rep'), may hold values from -6 to 6
- self_gain: float32 [768], P('fsdp'), may hold values from 0.5 to 1.5
- self_query: float32 [768, 768], P('fsdp'), may hold values from -0.02734375 to 0.02734375
- self_key: float32 [768, 768], P('fsdp'), may hold values from -0.21875 to 0.21875
- self_value: float32 [768, 768], P('fsdp'), may hold values from -0.21875 to 0.21875
- self_output: float32 [768, 768], P('fsdp'), may hold values from -1.75 to 1.75
- bucket_bias: float32 [384], P('fsdp'), may hold values from -3 to 3
- cross_gain: float32 [768], P('fsdp'), may hold values from 0.5 to 1.5
- cross_query: float32 [768, 768], P('fsdp'), may hold values from -0.02734375 to 0.02734375
- cross_key: float32 [768, 768], P('fsdp'), may hold values from -0.21875 to 0.21875
- cross_value: float32 [768, 768], P('fsdp'), may hold values from -0.21875 to 0.21875
- cross_output: float32 [768, 768], P('fsdp'), may hold values from -2.5 to 2.5
- feed_gain: float32 [768], P('fsdp'), may hold values from 0.5 to 1.5
- gate_weight: float32 [768, 2048], P('fsdp'), may hold values from -0.21875 to 0.21875
- up_weight: float32 [768, 2048], P('fsdp'), may hold values from -0.21875 to 0.21875
- down_weight: float32 [2048, 768], P('fsdp'), may hold values from -0.125 to 0.125
Outputs:
- output: float32 [8, 1024, 768], P('fsdp', 'rep')
- input_grad: float32 [8, 1024, 768], P('fsdp', 'rep')
- memory_grad: float32 [8, 3072, 768], P('fsdp', 'rep')
- self_gain_grad: float32 [768], P('fsdp')
- self_query_grad: float32 [768, 768], P('fsdp')
- self_key_grad: float32 [768, 768], P('fsdp')
- self_value_grad: float32 [768, 768], P('fsdp')
- self_output_grad: float32 [768, 768], P('fsdp')
- bucket_bias_grad: float32 [384], P('fsdp')
- cross_gain_grad: float32 [768], P('fsdp')
- cross_query_grad: float32 [768, 768], P('fsdp')
- cross_key_grad: float32 [768, 768], P('fsdp')
- cross_value_grad: float32 [768, 768], P('fsdp')
- cross_output_grad: float32 [768, 768], P('fsdp')
- feed_gain_grad: float32 [768], P('fsdp')
- gate_weight_grad: float32 [768, 2048], P('fsdp')
- up_weight_grad: float32 [768, 2048], P('fsdp')
- down_weight_grad: float32 [2048, 768], P('fsdp')
Inputs may be any that keep to these rules, and one draw needn't show every extreme that they name: `memory_lengths`: one sequence of all has exactly 3072. `distance_bucket`: Non-decreasing in the distance, 0 at distance 0 and 31 at distance 1024 - 1.
All inputs are finite; a program needn't handle non-finite values.
Results may differ from a plain program's by a relative error of at most 0.028.
Values may be sent and summed in bfloat16 or wider, within the bound.
No kernel may reach another device: no remote copies, remote signals or barrier semaphores. Data moves between devices by JAX's collectives and lax.ppermute only.
A program may use at most 256 MiB of HBM per device.

v0:
```python
import jax
import jax.numpy as jnp
from jax import lax
from jax.sharding import PartitionSpec as P

HEADS = 12
HEAD = 64
BUCKETS = 32


EPS = 1e-06
NEG = -1e30


def normalize(values, gain):
    inverse = lax.rsqrt(jnp.mean(values * values, -1, keepdims=True) + EPS)
    return values * inverse * gain


def project(inputs, weight):
    return jnp.dot(inputs, weight, preferred_element_type=jnp.float32)


def left_product(left, right):
    return lax.dot_general(
        left, right, (((0,), (0,)), ((), ())), preferred_element_type=jnp.float32
    )


def right_product(grad_rows, weight):
    return lax.dot_general(
        grad_rows, weight, (((1,), (1,)), ((), ())), preferred_element_type=jnp.float32
    )


def gelu_product(gate_value, up_value):
    return jax.nn.gelu(gate_value, approximate=True) * up_value


def raw_scores(query_rows, key_rows, bias, mask):
    key_four = key_rows.reshape(key_rows.shape[0], HEADS, HEAD)
    scores = jnp.einsum("rhd,khd->hrk", query_rows, key_four, preferred_element_type=jnp.float32)
    if bias is not None:
        scores = scores + bias
    return jnp.where(mask[None], scores, NEG)


def attend(queries, keys, values, bias, masks):

    def one_sequence(item):
        query_rows, key_rows, value_rows, mask = item
        scores = raw_scores(query_rows, key_rows, bias, mask)
        highest = jnp.max(scores, -1, keepdims=True)
        exponent = jnp.exp(scores - highest)
        row_total = jnp.sum(exponent, -1, keepdims=True)
        weights_soft = (exponent / row_total).astype(jnp.bfloat16)
        value_four = value_rows.reshape(value_rows.shape[0], HEADS, HEAD)
        mixed_heads = jnp.einsum(
            "hrk,khd->rhd", weights_soft, value_four, preferred_element_type=jnp.float32
        )
        flat_mixed = mixed_heads.reshape(query_rows.shape[0], HEADS * HEAD).astype(jnp.bfloat16)
        return (flat_mixed, highest + jnp.log(row_total))

    mixed, log_total = lax.map(one_sequence, (queries, keys, values, masks))
    return (mixed.reshape(mixed.shape[0] * mixed.shape[1], HEADS * HEAD), log_total)


def attend_back(queries, keys, values, bias, masks, log_total, grad_mixed):
    sequences, local_rows = (queries.shape[0], queries.shape[1])
    inner_width = HEADS * HEAD
    grad_four = grad_mixed.reshape(sequences, local_rows, HEADS, HEAD)

    def one_sequence(item):
        query_rows, key_rows, value_rows, mask, log_rows, grad_rows = item
        scores = raw_scores(query_rows, key_rows, bias, mask)
        weights_soft = jnp.exp(scores - log_rows)
        key_four = key_rows.reshape(key_rows.shape[0], HEADS, HEAD)
        value_four = value_rows.reshape(value_rows.shape[0], HEADS, HEAD)
        grad_weights = jnp.einsum(
            "rhd,khd->hrk", grad_rows, value_four, preferred_element_type=jnp.float32
        )
        grad_values = jnp.einsum(
            "hrk,rhd->khd",
            weights_soft.astype(jnp.bfloat16),
            grad_rows,
            preferred_element_type=jnp.float32,
        )
        inner_sum = jnp.sum(grad_weights * weights_soft, -1, keepdims=True)
        grad_scores = (weights_soft * (grad_weights - inner_sum)).astype(jnp.bfloat16)
        grad_queries = jnp.einsum(
            "hrk,khd->rhd", grad_scores, key_four, preferred_element_type=jnp.float32
        )
        grad_keys = jnp.einsum(
            "hrk,rhd->khd", grad_scores, query_rows, preferred_element_type=jnp.float32
        )
        flat = (
            grad_queries.reshape(local_rows, inner_width),
            grad_keys.reshape(key_rows.shape[0], inner_width),
            grad_values.reshape(key_rows.shape[0], inner_width),
        )
        if bias is None:
            return flat
        return flat + (grad_scores,)

    results = lax.map(one_sequence, (queries, keys, values, masks, log_total, grad_four))
    grad_scores = results[3] if bias is not None else None
    return (
        results[0].reshape(sequences * local_rows, inner_width),
        results[1],
        results[2],
        grad_scores,
    )


def bucket_hot(distance, distance_bucket, length_all):
    bucket_codes = jnp.arange(BUCKETS, dtype=jnp.int32)
    below = jnp.sum((distance_bucket[None, :] < bucket_codes[:, None]).astype(jnp.int32), 1)
    upper = jnp.sum((distance_bucket[None, :] <= bucket_codes[:, None]).astype(jnp.int32), 1)
    lower = jnp.where(bucket_codes == 0, -length_all, below)
    inside = (distance[None] >= lower[:, None, None]) & (distance[None] < upper[:, None, None])
    return inside.astype(jnp.bfloat16)


def per_device(
    decoder_input,
    memory,
    memory_lengths,
    distance_bucket,
    cotangent,
    self_gain,
    self_query,
    self_key,
    self_value,
    self_output,
    bucket_bias,
    cross_gain,
    cross_query,
    cross_key,
    cross_value,
    cross_output,
    feed_gain,
    gate_weight,
    up_weight,
    down_weight,
):
    masters = (
        self_gain,
        self_query,
        self_key,
        self_value,
        self_output,
        bucket_bias,
        cross_gain,
        cross_query,
        cross_key,
        cross_value,
        cross_output,
        feed_gain,
        gate_weight,
        up_weight,
        down_weight,
    )
    lowered = [weight.astype(jnp.bfloat16) for weight in masters]
    fetched = (
        lax.all_gather(lowered[0], "fsdp", axis=0, tiled=True),
        lax.all_gather(lowered[1], "fsdp", axis=0, tiled=True),
        lax.all_gather(lowered[2], "fsdp", axis=0, tiled=True),
        lax.all_gather(lowered[3], "fsdp", axis=0, tiled=True),
        lax.all_gather(lowered[4], "fsdp", axis=0, tiled=True),
        lax.all_gather(lowered[5], "fsdp", axis=0, tiled=True),
        lax.all_gather(lowered[6], "fsdp", axis=0, tiled=True),
        lax.all_gather(lowered[7], "fsdp", axis=0, tiled=True),
        lax.all_gather(lowered[8], "fsdp", axis=0, tiled=True),
        lax.all_gather(lowered[9], "fsdp", axis=0, tiled=True),
        lax.all_gather(lowered[10], "fsdp", axis=0, tiled=True),
        lax.all_gather(lowered[11], "fsdp", axis=0, tiled=True),
        lax.all_gather(lowered[12], "fsdp", axis=0, tiled=True),
        lax.all_gather(lowered[13], "fsdp", axis=0, tiled=True),
        lax.all_gather(lowered[14], "fsdp", axis=0, tiled=True),
    )
    (
        gain_one,
        query_one,
        key_one,
        value_one,
        output_one,
        table_flat,
        gain_two,
        query_two,
        key_two,
        value_two,
        output_two,
        gain_three,
        gate_matrix,
        up_matrix,
        down_matrix,
    ) = fetched
    sequences, local_rows, model_width = decoder_input.shape
    memory_rows = memory.shape[1]
    inner_width = HEADS * HEAD
    replicas = lax.axis_size("rep")
    length_all = local_rows * replicas
    memory_all = memory_rows * replicas
    memory_flat = memory.reshape(sequences * memory_rows, model_width)
    memory_keys = (
        project(memory_flat, key_two)
        .astype(jnp.bfloat16)
        .reshape(sequences, memory_rows, inner_width)
    )
    memory_values = (
        project(memory_flat, value_two)
        .astype(jnp.bfloat16)
        .reshape(sequences, memory_rows, inner_width)
    )
    cross_keys, cross_values = (
        lax.all_gather(memory_keys, "rep", axis=1, tiled=True),
        lax.all_gather(memory_values, "rep", axis=1, tiled=True),
    )
    reachable = (jnp.arange(memory_all, dtype=jnp.int32)[None, :] < memory_lengths[:, None])[
        :, None, :
    ]
    positions = lax.axis_index("rep") * local_rows + jnp.arange(local_rows, dtype=jnp.int32)
    distance = positions[:, None] - jnp.arange(length_all, dtype=jnp.int32)[None, :]
    causal = (distance >= 0)[None]
    place_hot = bucket_hot(distance, distance_bucket, length_all)
    bias_table = table_flat.reshape(HEADS, BUCKETS)
    bias = jnp.einsum("hb,brk->hrk", bias_table, place_hot, preferred_element_type=jnp.float32)
    inputs = decoder_input.astype(jnp.float32).reshape(sequences * local_rows, model_width)
    normed_one = normalize(inputs, gain_one.astype(jnp.float32)).astype(jnp.bfloat16)
    queries_one = (
        project(normed_one, query_one)
        .astype(jnp.bfloat16)
        .reshape(sequences, local_rows, HEADS, HEAD)
    )
    keys_local = (
        project(normed_one, key_one)
        .astype(jnp.bfloat16)
        .reshape(sequences, local_rows, inner_width)
    )
    values_local = (
        project(normed_one, value_one)
        .astype(jnp.bfloat16)
        .reshape(sequences, local_rows, inner_width)
    )
    self_keys_all, self_values_all = (
        lax.all_gather(keys_local, "rep", axis=1, tiled=True),
        lax.all_gather(values_local, "rep", axis=1, tiled=True),
    )
    mixed_one, log_total_one = attend(queries_one, self_keys_all, self_values_all, bias, causal)
    middle = inputs + project(mixed_one, output_one)
    normed_two = normalize(middle, gain_two.astype(jnp.float32)).astype(jnp.bfloat16)
    queries_two = (
        project(normed_two, query_two)
        .astype(jnp.bfloat16)
        .reshape(sequences, local_rows, HEADS, HEAD)
    )
    mixed_two, log_total_two = attend(queries_two, cross_keys, cross_values, None, reachable)
    after_cross = middle + project(mixed_two, output_two)
    normed_three = normalize(after_cross, gain_three.astype(jnp.float32)).astype(jnp.bfloat16)
    gate_value = project(normed_three, gate_matrix)
    up_value = project(normed_three, up_matrix)
    hidden = gelu_product(gate_value, up_value).astype(jnp.bfloat16)
    output = after_cross + project(hidden, down_matrix)
    backing = (
        lax.all_gather(lowered[0], "fsdp", axis=0, tiled=True),
        lax.all_gather(lowered[1], "fsdp", axis=0, tiled=True),
        lax.all_gather(lowered[2], "fsdp", axis=0, tiled=True),
        lax.all_gather(lowered[3], "fsdp", axis=0, tiled=True),
        lax.all_gather(lowered[4], "fsdp", axis=0, tiled=True),
        lax.all_gather(lowered[5], "fsdp", axis=0, tiled=True),
        lax.all_gather(lowered[6], "fsdp", axis=0, tiled=True),
        lax.all_gather(lowered[7], "fsdp", axis=0, tiled=True),
        lax.all_gather(lowered[8], "fsdp", axis=0, tiled=True),
        lax.all_gather(lowered[9], "fsdp", axis=0, tiled=True),
        lax.all_gather(lowered[10], "fsdp", axis=0, tiled=True),
        lax.all_gather(lowered[11], "fsdp", axis=0, tiled=True),
        lax.all_gather(lowered[12], "fsdp", axis=0, tiled=True),
        lax.all_gather(lowered[13], "fsdp", axis=0, tiled=True),
        lax.all_gather(lowered[14], "fsdp", axis=0, tiled=True),
    )
    (
        gain_one,
        query_one,
        key_one,
        value_one,
        output_one,
        table_flat,
        gain_two,
        query_two,
        key_two,
        value_two,
        output_two,
        gain_three,
        gate_matrix,
        up_matrix,
        down_matrix,
    ) = backing
    grad_output = cotangent.reshape(sequences * local_rows, model_width)
    grad_branch = grad_output.astype(jnp.bfloat16)
    grad_down = left_product(hidden, grad_branch)
    grad_hidden = right_product(grad_branch, down_matrix)
    gelu_value, gelu_pull = jax.vjp(gelu_product, gate_value, up_value)
    grad_gate_value, grad_up_value = gelu_pull(grad_hidden)
    grad_gate_low = grad_gate_value.astype(jnp.bfloat16)
    grad_up_low = grad_up_value.astype(jnp.bfloat16)
    grad_gate = left_product(normed_three, grad_gate_low)
    grad_up = left_product(normed_three, grad_up_low)
    grad_normed_three = right_product(grad_gate_low, gate_matrix) + right_product(
        grad_up_low, up_matrix
    )
    norm_value, norm_pull = jax.vjp(normalize, after_cross, gain_three.astype(jnp.float32))
    grad_after_part, grad_gain_three = norm_pull(grad_normed_three)
    grad_after = grad_output + grad_after_part
    grad_cross_branch = grad_after.astype(jnp.bfloat16)
    grad_output_two = left_product(mixed_two, grad_cross_branch)
    grad_mixed_two = right_product(grad_cross_branch, output_two).astype(jnp.bfloat16)
    grad_queries_two, grad_keys_two, grad_values_two, unused_scores = attend_back(
        queries_two, cross_keys, cross_values, None, reachable, log_total_two, grad_mixed_two
    )
    keys_two_low = grad_keys_two.astype(jnp.bfloat16)
    values_two_low = grad_values_two.astype(jnp.bfloat16)
    parted_keys = keys_two_low.reshape(sequences, replicas, memory_rows, inner_width)
    parted_values = values_two_low.reshape(sequences, replicas, memory_rows, inner_width)
    owned_keys, owned_values = (
        lax.all_to_all(parted_keys, "rep", split_axis=1, concat_axis=1, tiled=True),
        lax.all_to_all(parted_values, "rep", split_axis=1, concat_axis=1, tiled=True),
    )
    keys_two_flat = owned_keys.reshape(sequences * replicas * memory_rows, inner_width)
    values_two_flat = owned_values.reshape(sequences * replicas * memory_rows, inner_width)
    memory_terms = right_product(keys_two_flat, key_two) + right_product(values_two_flat, value_two)
    grad_memory = jnp.sum(
        memory_terms.reshape(sequences, replicas, memory_rows, model_width), 1
    ).reshape(sequences * memory_rows, model_width)
    memory_repeat = jnp.broadcast_to(
        memory[:, None], (sequences, replicas, memory_rows, model_width)
    ).reshape(sequences * replicas * memory_rows, model_width)
    grad_key_two = left_product(memory_repeat, keys_two_flat)
    grad_value_two = left_product(memory_repeat, values_two_flat)
    grad_queries_two_low = grad_queries_two.astype(jnp.bfloat16)
    grad_query_two = left_product(normed_two, grad_queries_two_low)
    grad_normed_two = right_product(grad_queries_two_low, query_two)
    norm_value, norm_pull = jax.vjp(normalize, middle, gain_two.astype(jnp.float32))
    grad_middle_part, grad_gain_two = norm_pull(grad_normed_two)
    grad_middle = grad_after + grad_middle_part
    grad_self_branch = grad_middle.astype(jnp.bfloat16)
    grad_output_one = left_product(mixed_one, grad_self_branch)
    grad_mixed_one = right_product(grad_self_branch, output_one).astype(jnp.bfloat16)
    grad_queries_one, grad_keys_one, grad_values_one, grad_scores_one = attend_back(
        queries_one, self_keys_all, self_values_all, bias, causal, log_total_one, grad_mixed_one
    )
    grad_table = jnp.einsum(
        "shrk,brk->hb", grad_scores_one, place_hot, preferred_element_type=jnp.float32
    ).reshape(HEADS * BUCKETS)
    keys_one_low = grad_keys_one.astype(jnp.bfloat16)
    values_one_low = grad_values_one.astype(jnp.bfloat16)
    grad_queries_one_low = grad_queries_one.astype(jnp.bfloat16)
    parted_keys_one = keys_one_low.reshape(sequences, replicas, local_rows, inner_width)
    parted_values_one = values_one_low.reshape(sequences, replicas, local_rows, inner_width)
    owned_keys_one, owned_values_one = (
        lax.all_to_all(parted_keys_one, "rep", split_axis=1, concat_axis=1, tiled=True),
        lax.all_to_all(parted_values_one, "rep", split_axis=1, concat_axis=1, tiled=True),
    )
    keys_one_flat = owned_keys_one.reshape(sequences * replicas * local_rows, inner_width)
    values_one_flat = owned_values_one.reshape(sequences * replicas * local_rows, inner_width)
    normed_terms = right_product(keys_one_flat, key_one) + right_product(values_one_flat, value_one)
    grad_normed_kv = jnp.sum(
        normed_terms.reshape(sequences, replicas, local_rows, model_width), 1
    ).reshape(sequences * local_rows, model_width)
    normed_repeat = jnp.broadcast_to(
        normed_one.reshape(sequences, 1, local_rows, model_width),
        (sequences, replicas, local_rows, model_width),
    ).reshape(sequences * replicas * local_rows, model_width)
    grad_key_one = left_product(normed_repeat, keys_one_flat)
    grad_value_one = left_product(normed_repeat, values_one_flat)
    grad_query_one = left_product(normed_one, grad_queries_one_low)
    grad_normed_one = right_product(grad_queries_one_low, query_one) + grad_normed_kv
    norm_value, norm_pull = jax.vjp(normalize, inputs, gain_one.astype(jnp.float32))
    grad_input_part, grad_gain_one = norm_pull(grad_normed_one)
    grad_input = grad_middle + grad_input_part
    scattered = (
        lax.psum_scatter(grad_gain_one, "fsdp", scatter_dimension=0, tiled=True),
        lax.psum_scatter(grad_query_one, "fsdp", scatter_dimension=0, tiled=True),
        lax.psum_scatter(grad_key_one, "fsdp", scatter_dimension=0, tiled=True),
        lax.psum_scatter(grad_value_one, "fsdp", scatter_dimension=0, tiled=True),
        lax.psum_scatter(grad_output_one, "fsdp", scatter_dimension=0, tiled=True),
        lax.psum_scatter(grad_table, "fsdp", scatter_dimension=0, tiled=True),
        lax.psum_scatter(grad_gain_two, "fsdp", scatter_dimension=0, tiled=True),
        lax.psum_scatter(grad_query_two, "fsdp", scatter_dimension=0, tiled=True),
        lax.psum_scatter(grad_key_two, "fsdp", scatter_dimension=0, tiled=True),
        lax.psum_scatter(grad_value_two, "fsdp", scatter_dimension=0, tiled=True),
        lax.psum_scatter(grad_output_two, "fsdp", scatter_dimension=0, tiled=True),
        lax.psum_scatter(grad_gain_three, "fsdp", scatter_dimension=0, tiled=True),
        lax.psum_scatter(grad_gate, "fsdp", scatter_dimension=0, tiled=True),
        lax.psum_scatter(grad_up, "fsdp", scatter_dimension=0, tiled=True),
        lax.psum_scatter(grad_down, "fsdp", scatter_dimension=0, tiled=True),
    )
    summed = (
        lax.psum(scattered[0].astype(jnp.bfloat16), "rep").astype(jnp.float32),
        lax.psum(scattered[1].astype(jnp.bfloat16), "rep").astype(jnp.float32),
        lax.psum(scattered[2].astype(jnp.bfloat16), "rep").astype(jnp.float32),
        lax.psum(scattered[3].astype(jnp.bfloat16), "rep").astype(jnp.float32),
        lax.psum(scattered[4].astype(jnp.bfloat16), "rep").astype(jnp.float32),
        lax.psum(scattered[5].astype(jnp.bfloat16), "rep").astype(jnp.float32),
        lax.psum(scattered[6].astype(jnp.bfloat16), "rep").astype(jnp.float32),
        lax.psum(scattered[7].astype(jnp.bfloat16), "rep").astype(jnp.float32),
        lax.psum(scattered[8].astype(jnp.bfloat16), "rep").astype(jnp.float32),
        lax.psum(scattered[9].astype(jnp.bfloat16), "rep").astype(jnp.float32),
        lax.psum(scattered[10].astype(jnp.bfloat16), "rep").astype(jnp.float32),
        lax.psum(scattered[11].astype(jnp.bfloat16), "rep").astype(jnp.float32),
        lax.psum(scattered[12].astype(jnp.bfloat16), "rep").astype(jnp.float32),
        lax.psum(scattered[13].astype(jnp.bfloat16), "rep").astype(jnp.float32),
        lax.psum(scattered[14].astype(jnp.bfloat16), "rep").astype(jnp.float32),
    )
    return (
        output.reshape(sequences, local_rows, model_width),
        grad_input.reshape(sequences, local_rows, model_width),
        grad_memory.reshape(sequences, memory_rows, model_width),
        summed[0],
        summed[1],
        summed[2],
        summed[3],
        summed[4],
        summed[5],
        summed[6],
        summed[7],
        summed[8],
        summed[9],
        summed[10],
        summed[11],
        summed[12],
        summed[13],
        summed[14],
    )


def solution(mesh):
    return jax.shard_map(
        per_device,
        mesh=mesh,
        in_specs=(
            P("fsdp", "rep", None),
            P("fsdp", "rep", None),
            P("fsdp"),
            P(),
            P("fsdp", "rep", None),
            P("fsdp"),
            P("fsdp", None),
            P("fsdp", None),
            P("fsdp", None),
            P("fsdp", None),
            P("fsdp"),
            P("fsdp"),
            P("fsdp", None),
            P("fsdp", None),
            P("fsdp", None),
            P("fsdp", None),
            P("fsdp"),
            P("fsdp", None),
            P("fsdp", None),
            P("fsdp", None),
        ),
        out_specs=(
            P("fsdp", "rep", None),
            P("fsdp", "rep", None),
            P("fsdp", "rep", None),
            P("fsdp"),
            P("fsdp", None),
            P("fsdp", None),
            P("fsdp", None),
            P("fsdp", None),
            P("fsdp"),
            P("fsdp"),
            P("fsdp", None),
            P("fsdp", None),
            P("fsdp", None),
            P("fsdp", None),
            P("fsdp"),
            P("fsdp", None),
            P("fsdp", None),
            P("fsdp", None),
        ),
        check_vma=False,
    )
```

profile of v0, /device:TPU:0, one launch (start us, length us, event | category | flops | bytes accessed | tf_op | source)
XLA Modules:
  0.0 1788.0 jit_solution(7910475163225129716)
XLA Ops:
  22.0 23.5 %all-reduce.9 = (bf16[768]{0:T(1024)(128)(2,1)S(1)}, bf16[384]{0:T(512)(128)(2,1)S(1)}, bf16[768]{0:T(1024)(128)(2,1)S(1)}, bf16[768]{0:T(1024)(128)(2,1)S(1)}) all-reduce(bf16[768]{0:T(1024)(128)(2,1)S(1)} %dynamic-update-slice, bf16[384]{0:T(512)(128)(2,1)S(1)} %dynamic-update-slice.1, ...), channel_id=1, replica_groups=mesh['rep'=4,'fsdp'=8] {'fsdp'}, use_global_device_ids=true, to_apply=%add | all-reduce | flops 2688 | bytes 10752
  57.3 40.0 %all-gather.20.cloned.1.call-done = bf16[768,768]{1,0:T(8,128)(2,1)} async-done(((bf16[96,768]{1,0:T(8,128)(2,1)}), bf16[768,768]{1,0:T(8,128)(2,1)}) %all-gather.20.cloned.1.call-update) | async-done | bytes 1179664 | tf_op jit(solution)/shard_map/all_gather | solution.py:168
  101.3 38.5 %all-gather.32.cloned.1.call-done = bf16[768,768]{1,0:T(8,128)(2,1)} async-done(((bf16[96,768]{1,0:T(8,128)(2,1)}), bf16[768,768]{1,0:T(8,128)(2,1)}) %all-gather.32.cloned.1.call-update) | async-done | bytes 1179664 | tf_op jit(solution)/shard_map/all_gather | solution.py:173
  143.3 39.0 %all-gather.28.cloned.1.call-done = bf16[768,768]{1,0:T(8,128)(2,1)} async-done(((bf16[96,768]{1,0:T(8,128)(2,1)}), bf16[768,768]{1,0:T(8,128)(2,1)}) %all-gather.28.cloned.1.call-update) | async-done | bytes 1179664 | tf_op jit(solution)/shard_map/all_gather | solution.py:174
  202.6 47.5 %copy.111 = pred[32,256,1024]{2,0,1:T(32,128)(4,1)} copy(pred[32,256,1024]{1,0,2:T(32,128)(4,1)S(1)} %compare_and_fusion) | data formatting | bytes 16777216 | tf_op jit(solution)/shard_map/and | solution.py:120
  250.8 13.2 fusion.105
  268.8 15.5 fusion.99
  298.6 12.3 all-gather.26.cloned.1.call-done
  312.8 40.7 %all-gather.30.cloned.1.call-done = bf16[768,768]{1,0:T(8,128)(2,1)} async-done(((bf16[96,768]{1,0:T(8,128)(2,1)}), bf16[768,768]{1,0:T(8,128)(2,1)}) %all-gather.30.cloned.1.call-update) | async-done | bytes 1179664 | tf_op jit(solution)/shard_map/all_gather | solution.py:172
  355.5 35.7 %all-gather.48.cloned.1.call-done = bf16[3072,768]{1,0:T(8,128)(2,1)} async-done(((bf16[768,768]{1,0:T(8,128)(2,1)}), bf16[3072,768]{1,0:T(8,128)(2,1)}) %all-gather.48.cloned.1.call-update) | async-done | bytes 4718608 | tf_op jit(solution)/shard_map/all_gather | solution.py:216
  397.9 17.7 select_reduce_fusion
  415.5 15.9 fusion
  438.1 16.5 fusion.56
  454.6 19.9 %all-gather.34.cloned.1.call-done = bf16[768,768]{1,0:T(8,128)(2,1)} async-done(((bf16[96,768]{1,0:T(8,128)(2,1)}), bf16[768,768]{1,0:T(8,128)(2,1)}) %all-gather.34.cloned.1.call-update) | async-done | bytes 1179664 | tf_op jit(solution)/shard_map/all_gather | solution.py:175
  476.6 60.0 %all-gather.36.cloned.1.call-done = bf16[768,2048]{1,0:T(8,128)(2,1)} async-done(((bf16[96,2048]{1,0:T(8,128)(2,1)}), bf16[768,2048]{1,0:T(8,128)(2,1)}) %all-gather.36.cloned.1.call-update) | async-done | bytes 3145744 | tf_op jit(solution)/shard_map/all_gather | solution.py:177
  540.7 57.5 %all-gather.38.cloned.1.call-done = bf16[768,2048]{1,0:T(8,128)(2,1)} async-done(((bf16[96,2048]{1,0:T(8,128)(2,1)}), bf16[768,2048]{1,0:T(8,128)(2,1)}) %all-gather.38.cloned.1.call-update) | async-done | bytes 3145744 | tf_op jit(solution)/shard_map/all_gather | solution.py:178
  602.5 57.5 %all-gather.40.cloned.1.call-done = bf16[2048,768]{1,0:T(8,128)(2,1)} async-done(((bf16[256,768]{1,0:T(8,128)(2,1)}), bf16[2048,768]{1,0:T(8,128)(2,1)}) %all-gather.40.cloned.1.call-update) | async-done | bytes 3145744 | tf_op jit(solution)/shard_map/all_gather | solution.py:179
  673.2 27.3 %multiply_reduce_fusion = (f32[12,256]{1,0:T(8,128)S(1)}, f32[12,256,3072]{2,1,0:T(8,128)}) fusion(f32[12,256,3072]{2,1,0:T(8,128)} %get-tuple-element.242, f32[12,256]{1,0:T(8,128)S(1)} %log_add_fusion.1, pred[3072]{0:T(1024)(128)(4,1)S(1)} %copy-done.51, bf16[256,12,64]{0,2,1:T(8,128)(2,1)S(1)} %bitcast.228, bf16[3072,12,64]{0,2,1:T(8,128)(2,1)} %bitcast.223), kind=kOutput, calls=%fused_computation.1 | convolution fusion | flops 1245705216 | bytes 80636928 | tf_op jit(solution)/shard_map/while/body/eval_jaxpr/rhd,khd->hrk/dot_general | solution.py:79
  700.5 31.2 %multiply_convert_fusion = bf16[12,256,3072]{2,1,0:T(8,128)(2,1)} fusion(f32[12,256,3072]{2,1,0:T(8,128)} %get-tuple-element.247, f32[12,256,3072]{2,1,0:T(8,128)} %get-tuple-element.242, f32[12,256]{1,0:T(8,128)S(1)} %get-tuple-element.246, f32[12,256]{1,0:T(8,128)S(1)} %log_add_fusion.1, pred[3072]{0:T(1024)(128)(4,1)S(1)} %copy-done.51), kind=kLoop, calls=%fused_computation | loop fusion | flops 47185920 | bytes 94399488 | tf_op jit(solution)/shard_map/while/body/eval_jaxpr/convert_element_type | solution.py:89
  798.6 19.9 %all-to-all-done = bf16[1,4,256,768]{3,2,0,1:T(8,128)(2,1)} async-done(((bf16[1,4,256,768]{3,2,0,1:T(8,128)(2,1)}), bf16[1,4,256,768]{3,2,0,1:T(8,128)(2,1)}, u32[]{:S(2)}, u32[]{:S(2)}) %all-to-all-start) | async-done | bytes 1572896 | tf_op jit(solution)/shard_map/all_to_all | solution.py:360
  839.0 23.6 %all_to_all.20 = bf16[1,4,256,768]{3,2,0,1:T(8,128)(2,1)S(1)} all-to-all(bf16[1,4,256,768]{3,2,0,1:T(8,128)(2,1)} %copy.119), channel_id=1, replica_groups=mesh['rep'=4,'fsdp'=8] {'rep'}, dimensions={1} | all-to-all | bytes 3145728 | tf_op jit(solution)/shard_map/all_to_all | solution.py:361
  891.4 56.4 %all_to_all.21 = bf16[1,4,768,768]{2,3,0,1:T(8,128)(2,1)S(1)} all-to-all(bf16[1,4,768,768]{2,3,0,1:T(8,128)(2,1)S(1)} %copy.120), channel_id=1, replica_groups=mesh['rep'=4,'fsdp'=8] {'rep'}, dimensions={1} | all-to-all | bytes 9437184 | tf_op jit(solution)/shard_map/all_to_all | solution.py:325
  958.3 18.0 %fusion.23 = bf16[3072,12,64]{0,2,1:T(8,128)(2,1)} fusion(bf16[256,12,64]{0,2,1:T(8,128)(2,1)S(1)} %bitcast.229, f32[12,256,3072]{2,1,0:T(8,128)} %get-tuple-element.242, f32[12,256]{1,0:T(8,128)S(1)} %log_add_fusion.1, pred[3072]{0:T(1024)(128)(4,1)S(1)} %copy-done.52), kind=kOutput, calls=%fused_computation.34 | convolution fusion | flops 1238630400 | bytes 42875904 | tf_op jit(solution)/shard_map/while/body/eval_jaxpr/hrk,rhd->khd/dot_general | solution.py:82
  989.0 56.4 %all_to_all.22 = bf16[1,4,768,768]{2,3,0,1:T(8,128)(2,1)S(1)} all-to-all(bf16[1,4,768,768]{2,3,0,1:T(8,128)(2,1)S(1)} %copy.122), channel_id=1, replica_groups=mesh['rep'=4,'fsdp'=8] {'rep'}, dimensions={1} | all-to-all | bytes 9437184 | tf_op jit(solution)/shard_map/all_to_all | solution.py:326
  1073.3 12.3 copy.125
  1112.8 34.8 %all-reduce.8 = (bf16[768]{0:T(1024)(128)(2,1)S(1)}, bf16[384]{0:T(512)(128)(2,1)S(1)}, bf16[768]{0:T(1024)(128)(2,1)S(1)}, bf16[768]{0:T(1024)(128)(2,1)S(1)}) all-reduce(f32[768]{0:T(1024)S(1)} %get-tuple-element.205, f32[384]{0:T(512)S(1)} %reshape.447, f32[768]{0:T(1024)S(1)} %copy-done.65, ...), channel_id=6, replica_groups=mesh['rep'=4,'fsdp'=8] {'fsdp'}, use_global_device_ids=true, to_apply=%region_17.18.clone | all-reduce | flops 2688 | bytes 16128
  1198.5 70.3 %reduce-scatter.34.cloned.1.call-done = f32[96,768]{1,0:T(8,128)} async-done(((f32[768,768]{1,0:T(8,128)}), f32[96,768]{1,0:T(8,128)}) %reduce-scatter.34.cloned.1.call-update) | async-done | bytes 294928
  1270.6 70.0 %reduce-scatter.36.cloned.1.call-done = f32[96,768]{1,0:T(8,128)} async-done(((f32[768,768]{1,0:T(8,128)}), f32[96,768]{1,0:T(8,128)}) %reduce-scatter.36.cloned.1.call-update) | async-done | bytes 294928
  1342.3 118.7 %reduce-scatter.28.cloned.1.call-done = f32[96,2048]{1,0:T(8,128)} async-done(((f32[768,2048]{1,0:T(8,128)}), f32[96,2048]{1,0:T(8,128)}) %reduce-scatter.28.cloned.1.call-update) | async-done | bytes 786448 | tf_op jit(solution)/shard_map/reduce_scatter | solution.py:393
  1462.9 118.8 %reduce-scatter.30.cloned.1.call-done = f32[96,2048]{1,0:T(8,128)} async-done(((f32[768,2048]{1,0:T(8,128)}), f32[96,2048]{1,0:T(8,128)}) %reduce-scatter.30.cloned.1.call-update) | async-done | bytes 786448 | tf_op jit(solution)/shard_map/reduce_scatter | solution.py:394
  1583.7 118.7 %reduce-scatter.32.cloned.1.call-done = f32[256,768]{1,0:T(8,128)} async-done(((f32[2048,768]{1,0:T(8,128)}), f32[256,768]{1,0:T(8,128)}) %reduce-scatter.32.cloned.1.call-update) | async-done | bytes 786448 | tf_op jit(solution)/shard_map/reduce_scatter | solution.py:395
  1722.5 42.9 %all-reduce.14.cloned.1.call-done = (bf16[96,768]{1,0:T(8,128)(2,1)}, bf16[96,768]{1,0:T(8,128)(2,1)}, bf16[96,768]{1,0:T(8,128)(2,1)}, bf16[96,768]{1,0:T(8,128...) async-done(((bf16[96,768]{1,0:T(8,128)(2,1)}, ...) | async-done | bytes 2359312 | tf_op jit(solution)/shard_map/psum | solution.py:399
  (367 shorter events, 399.0 us)
Async XLA Ops:
  7.2 47.5 %all-gather.24.cloned.1.call-start = ((), (), s32[]{:S(2)}) async-start(), calls=%async_computation.17 | async-start | bytes 1327104 | tf_op jit(solution)/shard_map/all_gather | solution.py:167
  9.1 88.2 %all-gather.20.cloned.1.call-start = ((), (), s32[]{:S(2)}) async-start(), calls=%async_computation.15 | async-start | bytes 1327104 | tf_op jit(solution)/shard_map/all_gather | solution.py:168
  10.8 129.1 %all-gather.32.cloned.1.call-start = ((), (), s32[]{:S(2)}) async-start(), calls=%async_computation.21 | async-start | bytes 1327104 | tf_op jit(solution)/shard_map/all_gather | solution.py:173
  12.5 169.8 %all-gather.28.cloned.1.call-start = ((), (), s32[]{:S(2)}) async-start(), calls=%async_computation.19 | async-start | bytes 1327104 | tf_op jit(solution)/shard_map/all_gather | solution.py:174
  14.2 249.8 %all-gather.22.cloned.1.call-start = ((), (), s32[]{:S(2)}) async-start(), calls=%async_computation.16 | async-start | bytes 1327104 | tf_op jit(solution)/shard_map/all_gather | solution.py:166
  15.9 250.1 %all-gather.44.cloned.1.call-start = ((), (), s32[]{:S(2)}) async-start(), calls=%async_computation.36 | async-start | bytes 1966080 | tf_op jit(solution)/shard_map/all_gather | solution.py:246
  46.0 218.1 %copy-start.16 = (bf16[256,768]{1,0:T(8,128)(2,1)}, bf16[256,768]{1,0:T(8,128)(2,1)S(1)}, u32[]{:S(2)}) copy-start(bf16[256,768]{1,0:T(8,128)(2,1)S(1)} %fusion.63) | copy-start | bytes 1179652
  57.2 232.1 %all-gather.42.cloned.1.call-start = ((), (), s32[]{:S(2)}) async-start(), calls=%async_computation.35 | async-start | bytes 1966080 | tf_op jit(solution)/shard_map/all_gather | solution.py:247
  99.7 211.2 %all-gather.26.cloned.1.call-start = ((), (), s32[]{:S(2)}) async-start(), calls=%async_computation.18 | async-start | bytes 1327104 | tf_op jit(solution)/shard_map/all_gather | solution.py:169
  100.5 253.0 %all-gather.30.cloned.1.call-start = ((), (), s32[]{:S(2)}) async-start(), calls=%async_computation.20 | async-start | bytes 1327104 | tf_op jit(solution)/shard_map/all_gather | solution.py:172
  101.3 289.9 %all-gather.48.cloned.1.call-start = ((), (), s32[]{:S(2)}) async-start(), calls=%async_computation.38 | async-start | bytes 5898240 | tf_op jit(solution)/shard_map/all_gather | solution.py:216
  143.3 288.2 %all-gather.46.cloned.1.call-start = ((), (), s32[]{:S(2)}) async-start(), calls=%async_computation.37 | async-start | bytes 5898240 | tf_op jit(solution)/shard_map/all_gather | solution.py:217
  185.7 288.8 %all-gather.34.cloned.1.call-start = ((), (), s32[]{:S(2)}) async-start(), calls=%async_computation.22 | async-start | bytes 1327104 | tf_op jit(solution)/shard_map/all_gather | solution.py:175
  186.5 350.1 %all-gather.36.cloned.1.call-start = ((), (), s32[]{:S(2)}) async-start(), calls=%async_computation.23 | async-start | bytes 3538944 | tf_op jit(solution)/shard_map/all_gather | solution.py:177
  187.3 410.9 %all-gather.38.cloned.1.call-start = ((), (), s32[]{:S(2)}) async-start(), calls=%async_computation.24 | async-start | bytes 3538944 | tf_op jit(solution)/shard_map/all_gather | solution.py:178
  189.3 470.6 %all-gather.40.cloned.1.call-start = ((), (), s32[]{:S(2)}) async-start(), calls=%async_computation.25 | async-start | bytes 3538944 | tf_op jit(solution)/shard_map/all_gather | solution.py:179
  191.3 989.3 %reduce-scatter.16.cloned.1.call-start = ((), (), s32[]{:S(2)}) async-start(), calls=%async_computation.26 | async-start | bytes 2654208 | tf_op jit(solution)/shard_map/reduce_scatter | solution.py:382
  250.8 187.4 %copy-start.50 = (pred[3072]{0:T(1024)(128)(4,1)}, pred[3072]{0:T(1024)(128)(4,1)S(1)}, u32[]{:S(2)}) copy-start(pred[3072]{0:T(1024)(128)(4,1)S(1)} %iota_compare_fusion.2) | copy-start | bytes 9220
  476.4 194.8 %copy-start.12 = (f32[256,768]{1,0:T(8,128)}, f32[256,768]{1,0:T(8,128)S(1)}, u32[]{:S(2)}) copy-start(f32[256,768]{1,0:T(8,128)S(1)} %get-tuple-element.244) | copy-start | bytes 2359300
  771.8 410.5 %reduce-scatter.22.cloned.1.call-start = ((), (), s32[]{:S(2)}) async-start(), calls=%async_computation.29 | async-start | bytes 2654208 | tf_op jit(solution)/shard_map/reduce_scatter | solution.py:385
  774.7 409.2 %reduce-scatter.24.cloned.1.call-start = ((), (), s32[]{:S(2)}) async-start(), calls=%async_computation.30 | async-start | bytes 2654208 | tf_op jit(solution)/shard_map/reduce_scatter | solution.py:388
  777.8 407.7 %reduce-scatter.26.cloned.1.call-start = ((), (), s32[]{:S(2)}) async-start(), calls=%async_computation.31 | async-start | bytes 2654208 | tf_op jit(solution)/shard_map/reduce_scatter | solution.py:391
  794.0 24.5 %all-to-all-start = ((bf16[1,4,256,768]{3,2,0,1:T(8,128)(2,1)}), bf16[1,4,256,768]{3,2,0,1:T(8,128)(2,1)}, u32[]{:S(2)}, u32[]{:S(2)}) async-start(bf16[1,4,256,768]{3,2,0,1:T(8,128)(2,1)} %copy.118), calls=%async_computation | async-start | bytes 3145728 | tf_op jit(solution)/shard_map/all_to_all | solution.py:360
  798.4 388.8 %reduce-scatter.18.cloned.1.call-start = ((), (), s32[]{:S(2)}) async-start(), calls=%async_computation.27 | async-start | bytes 2654208 | tf_op jit(solution)/shard_map/reduce_scatter | solution.py:383
  822.8 374.1 %reduce-scatter.20.cloned.1.call-start = ((), (), s32[]{:S(2)}) async-start(), calls=%async_computation.28 | async-start | bytes 2654208 | tf_op jit(solution)/shard_map/reduce_scatter | solution.py:384
  866.6 402.2 %reduce-scatter.34.cloned.1.call-start = ((), (), s32[]{:S(2)}) async-start(), calls=%async_computation.39 | async-start | bytes 2654208
  958.2 382.3 %reduce-scatter.36.cloned.1.call-start = ((), (), s32[]{:S(2)}) async-start(), calls=%async_computation.40 | async-start | bytes 2654208
  1056.0 405.0 %reduce-scatter.28.cloned.1.call-start = ((), (), s32[]{:S(2)}) async-start(), calls=%async_computation.32 | async-start | bytes 7077888 | tf_op jit(solution)/shard_map/reduce_scatter | solution.py:393
  1061.0 520.8 %reduce-scatter.30.cloned.1.call-start = ((), (), s32[]{:S(2)}) async-start(), calls=%async_computation.33 | async-start | bytes 7077888 | tf_op jit(solution)/shard_map/reduce_scatter | solution.py:394
  1065.9 636.5 %reduce-scatter.32.cloned.1.call-start = ((), (), s32[]{:S(2)}) async-start(), calls=%async_computation.34 | async-start | bytes 7077888 | tf_op jit(solution)/shard_map/reduce_scatter | solution.py:395
  1071.9 693.5 %all-reduce.14.cloned.1.call-start = ((), (), s32[]{:S(2)}) async-start(), calls=%async_computation.41 | async-start | bytes 4915200 | tf_op jit(solution)/shard_map/psum | solution.py:399
  1270.6 433.8 %copy-start.71 = (bf16[768,768]{1,0:T(8,128)(2,1)S(1)}, bf16[768,768]{1,0:T(8,128)(2,1)}, u32[]{:S(2)}) copy-start(bf16[768,768]{1,0:T(8,128)(2,1)} %all-gather.28.cloned.1.call-done) | copy-start | bytes 3538948
  (72 other events, 1552.2 us)
Sparse Core Ops, SparseCore 0:
  10.8 43.8 all-gather.23
  57.4 39.7 all-gather.19
  100.0 39.8 all-gather.31
  142.4 39.8 all-gather.27
  184.9 39.8 all-gather.21
  226.7 18.4 all-gather.43
  247.3 19.6 all-gather.41
  269.8 41.0 all-gather.25
  313.6 39.8 all-gather.29
  354.9 36.2 all-gather.47
  393.3 37.4 all-gather.45
  433.4 41.0 all-gather.33
  477.3 59.2 all-gather.35
  539.1 59.0 all-gather.37
  600.8 59.0 all-gather.39
  771.9 67.4 reduce-scatter.15
  842.8 68.0 reduce-scatter.21
  914.2 67.9 reduce-scatter.23
  985.6 68.1 reduce-scatter.25
  1057.2 68.1 reduce-scatter.17
  1128.9 67.9 reduce-scatter.19
  1200.3 68.4 reduce-scatter.33
  1272.3 68.2 reduce-scatter.35
  1344.0 116.9 reduce-scatter.27
  1464.6 117.1 reduce-scatter.29
  1585.2 117.1 reduce-scatter.31
  1707.1 58.2 all-reduce.13
where the time goes:
time: 1800 us; the launch traced here: 1790 us
  waiting for transfers between devices  978 us (54%)
  matrix products  292 us (16%)
  blocking collectives  201 us (11%)
  local copies, waits for them, and re-layouts  167 us (9%)
  other arithmetic  126 us (7%)
  between operations  18.9 us (1%)
    unnamed x29, waiting for transfers between devices  141 us
    reduce_scatter x1, waiting for transfers between devices, per_device(): lax.psum_scatter(grad_up, 'fsdp', scatter_dimension=0, tiled=True)  119 us
    reduce_scatter x1, waiting for transfers between devices, per_device(): lax.psum_scatter(grad_gate, 'fsdp', scatter_dimension=0, tiled=True)  119 us
    reduce_scatter x1, waiting for transfers between devices, per_device(): lax.psum_scatter(grad_down, 'fsdp', scatter_dimension=0, tiled=True)  119 us
    all_gather x1, waiting for transfers between devices, per_device(): lax.all_gather(lowered[12], 'fsdp', axis=0, tiled=True)  60 us
    unnamed x2, blocking collectives  58.3 us
    all_gather x1, waiting for transfers between devices, per_device(): lax.all_gather(lowered[13], 'fsdp', axis=0, tiled=True)  57.5 us
    all_gather x1, waiting for transfers between devices, per_device(): lax.all_gather(lowered[14], 'fsdp', axis=0, tiled=True)  57.5 us
  transfers between devices with their start and end apart: 28, of which 19 were waited for; matrix products, arithmetic and copies ran while one was open for 25% of the time, Pallas kernels for 0%

commit v1 on v0

v1 whole, which is shorter than its diff:
```python
import functools

import jax
import jax.numpy as jnp
from jax import lax
from jax.experimental import pallas as pl
from jax.experimental.pallas import tpu as pltpu
from jax.sharding import PartitionSpec as P

HEAD = 64
BUCKETS = 32
EPS = 1e-06
NEG = -1e30
BF = jnp.bfloat16
F32 = jnp.float32
NN = (((1,), (0,)), ((), ()))
NT = (((1,), (1,)), ((), ()))
TN = (((0,), (0,)), ((), ()))
TT = (((0,), (1,)), ((), ()))

CORE = [(0, 1), (1, 0), (2, 3), (3, 2)]
FAR = [(0, 2), (2, 0), (1, 3), (3, 1)]


def core_swap(value):
    return lax.ppermute(value, "rep", CORE)


def far_swap(value):
    return lax.ppermute(value, "rep", FAR)


def dot(left, right, dims=NN):
    return lax.dot_general(left, right, dims, preferred_element_type=F32)


def half_rows(pair, head):
    row = lax.broadcasted_iota(jnp.int32, pair.shape, 0)
    keep = (row < HEAD) if head == 0 else (row >= HEAD)
    return jnp.where(keep, pair, jnp.zeros_like(pair))


def three_terms(value):
    first = value.astype(BF)
    rest = value - first.astype(F32)
    second = rest.astype(BF)
    third = (rest - second.astype(F32)).astype(BF)
    return first, second, third


def extra_rows(first_row, vector):
    terms = three_terms(-vector)
    row = lax.broadcasted_iota(jnp.int32, (128, vector.shape[1]), 0)
    out = jnp.where(row == 0, first_row, 0.0)
    for place, term in enumerate(terms):
        out = jnp.where(row == place + 1, term.astype(F32), out)
    return out.astype(BF)


def attend_kernel(chunk, biased, *refs):
    if biased:
        query, key, value, extra, bias, mixed, log_total = refs
    else:
        query, key, value, extra, mixed, log_total = refs
    keys, rows = key.shape[0], query.shape[1]
    pair = query[...]
    row = lax.broadcasted_iota(jnp.int32, (128, rows), 0)
    one = jnp.where(row == 0, 1.0, 0.0).astype(BF)
    wide = [half_rows(pair, h) for h in range(2)]
    if not biased:
        wide = [jnp.concatenate([w, one], 0) for w in wide]

    def score(part, head):
        span = pl.ds(part * chunk, chunk)
        if biased:
            return dot(key[span, :], wide[head]) + bias[head, span, :].astype(F32)
        return dot(jnp.concatenate([key[span, :], extra[span, :]], 1), wide[head])

    highest = [jnp.full((1, rows), NEG, F32)] * 2
    total = [jnp.zeros((1, rows), F32)] * 2
    acc = [jnp.zeros((HEAD, rows), F32)] * 2
    steps = [(part, head) for part in range(keys // chunk) for head in range(2)]
    ahead = score(*steps[0])
    for index, (part, head) in enumerate(steps):
        scores = ahead
        if index + 1 < len(steps):
            ahead = score(*steps[index + 1])
        span = pl.ds(part * chunk, chunk)
        top = jnp.maximum(highest[head], jnp.max(scores, 0, keepdims=True))
        soft = jnp.exp(scores - top)
        scale = jnp.exp(highest[head] - top)
        total[head] = total[head] * scale + jnp.sum(soft, 0, keepdims=True)
        product = dot(value[span, :], soft.astype(BF), TN)[head * HEAD : (head + 1) * HEAD]
        acc[head] = acc[head] * scale + product
        highest[head] = top
    for head in range(2):
        mixed[pl.ds(head * HEAD, HEAD), :] = (acc[head] / total[head]).astype(BF)
        log_total[0, pl.ds(head, 1), :] = highest[head] + jnp.log(total[head])


def attend(query, keyvalue, extra, bias=None, chunk=512):
    width, rows = query.shape
    keys = keyvalue.shape[0]
    pairs = width // 128
    across = pl.BlockSpec((128, rows), lambda p: (p, 0))
    in_specs = [
        across,
        pl.BlockSpec((keys, 128), lambda p: (0, p)),
        pl.BlockSpec((keys, 128), lambda p: (0, p + pairs)),
        pl.BlockSpec((keys, 128), lambda p: (0, 0)),
    ]
    args = [query, keyvalue, keyvalue, extra]
    if bias is not None:
        in_specs.append(pl.BlockSpec((2, keys, rows), lambda p: (p, 0, 0)))
        args.append(bias)
    return pl.pallas_call(
        functools.partial(attend_kernel, chunk, bias is not None),
        grid=(pairs,),
        in_specs=in_specs,
        out_specs=[across, pl.BlockSpec((1, 8, rows), lambda p: (p, 0, 0))],
        out_shape=[
            jax.ShapeDtypeStruct((width, rows), BF),
            jax.ShapeDtypeStruct((pairs, 8, rows), F32),
        ],
        compiler_params=pltpu.CompilerParams(vmem_limit_bytes=56 * 2**20),
        cost_estimate=pl.CostEstimate(
            flops=8 * keys * rows * width,
            bytes_accessed=4 * keys * width,
            transcendentals=keys * rows * width // HEAD,
        ),
    )(*args)


def attend_back_kernel(chunk, biased, *refs):
    if biased:
        query, key, value, extra, mixed, grad, log_total, bias, d_query, d_key, d_value, d_far = refs
    else:
        query, key, value, extra, mixed, grad, log_total, d_query, d_key, d_value = refs
    keys, rows = key.shape[0], query.shape[1]
    pair, grad_pair = query[...], grad[...]
    product = mixed[...].astype(F32) * grad_pair.astype(F32)
    q_half = [half_rows(pair, h) for h in range(2)]
    g_half = [half_rows(grad_pair, h) for h in range(2)]
    q_wide, g_wide = [], []
    for head in range(2):
        inner = jnp.sum(product[head * HEAD : (head + 1) * HEAD], 0, keepdims=True)
        logs = log_total[0, pl.ds(head, 1), :]
        q_wide.append(jnp.concatenate([q_half[head], extra_rows(1.0, logs)], 0))
        g_wide.append(jnp.concatenate([g_half[head], extra_rows(0.0, inner)], 0))
    if biased:
        block = 256
        down = lax.broadcasted_iota(jnp.int32, (block, block), 0)
        over = lax.broadcasted_iota(jnp.int32, (block, block), 1)
        flip = jnp.where(down + over == block - 1, 1.0, 0.0).astype(BF)
    acc = [jnp.zeros((HEAD, rows), F32) for _ in range(2)]
    for part in range(keys // chunk):
        span = pl.ds(part * chunk, chunk)
        key_wide = jnp.concatenate([key[span, :], extra[span, :]], 1)
        value_wide = jnp.concatenate([value[span, :], extra[span, :]], 1)
        dv, dk = 0.0, 0.0
        for head in range(2):
            scores = dot(key_wide, q_wide[head])
            if biased:
                scores = scores + bias[head, span, :].astype(F32)
            soft = jnp.exp(scores)
            d_scores = (soft * dot(value_wide, g_wide[head])).astype(BF)
            dv = dv + dot(soft.astype(BF), g_half[head], NT)
            dk = dk + dot(d_scores, q_half[head], NT)
            step = dot(key[span, :], d_scores, TN)[head * HEAD : (head + 1) * HEAD]
            acc[head] = acc[head] + step
            if biased:
                for j in range(chunk // block):
                    for i in range(rows // block):
                        tile = d_scores[j * block : (j + 1) * block, i * block : (i + 1) * block]
                        tile = jnp.concatenate([dot(flip, tile), jnp.zeros((block, block), F32)], 1)
                        tile = pltpu.roll(tile, 0, 1, stride=1, stride_axis=0)
                        place = (part * (chunk // block) + j) * (rows // block) + i
                        d_far[0, head, pl.ds(place, 1), :] = jnp.sum(tile, 0, keepdims=True)
        d_value[span, :] = dv.astype(BF)
        d_key[span, :] = dk.astype(BF)
    for head in range(2):
        d_query[pl.ds(head * HEAD, HEAD), :] = acc[head].astype(BF)


def attend_back(query, keyvalue, extra, mixed, grad, log_total, bias=None, chunk=512):
    width, rows = query.shape
    keys = keyvalue.shape[0]
    pairs = width // 128
    across = pl.BlockSpec((128, rows), lambda p: (p, 0))
    along = pl.BlockSpec((keys, 128), lambda p: (0, p))
    in_specs = [
        across,
        along,
        pl.BlockSpec((keys, 128), lambda p: (0, p + pairs)),
        pl.BlockSpec((keys, 128), lambda p: (0, 0)),
        across,
        across,
        pl.BlockSpec((1, 8, rows), lambda p: (p, 0, 0)),
    ]
    args = [query, keyvalue, keyvalue, extra, mixed, grad, log_total]
    out_specs = [across, along, along]
    out_shape = [
        jax.ShapeDtypeStruct((width, rows), BF),
        jax.ShapeDtypeStruct((keys, width), BF),
        jax.ShapeDtypeStruct((keys, width), BF),
    ]
    if bias is not None:
        in_specs.append(pl.BlockSpec((2, keys, rows), lambda p: (p, 0, 0)))
        args.append(bias)
        blocks = (keys // 256) * (rows // 256)
        out_specs.append(pl.BlockSpec((1, 2, blocks, 512), lambda p: (p, 0, 0, 0)))
        out_shape.append(jax.ShapeDtypeStruct((pairs, 2, blocks, 512), F32))
    return pl.pallas_call(
        functools.partial(attend_back_kernel, chunk, bias is not None),
        grid=(pairs,),
        in_specs=in_specs,
        out_specs=out_specs,
        out_shape=out_shape,
        compiler_params=pltpu.CompilerParams(vmem_limit_bytes=56 * 2**20),
        cost_estimate=pl.CostEstimate(
            flops=20 * keys * rows * width,
            bytes_accessed=8 * keys * width,
            transcendentals=keys * rows * width // HEAD,
        ),
    )(*args)


def bias_kernel(starts, line, out):
    head = pl.program_id(0)
    block = 256
    for j in range(4):
        for i in range(2):
            start = pl.multiple_of(starts[j * 2 + i], 128)
            row = line[pl.ds(head, 1), pl.ds(start, 2 * block)]
            tile = pltpu.roll(jnp.broadcast_to(row, (block, 2 * block)), 0, 1, stride=1, stride_axis=0)
            out[0, pl.ds(j * block, block), pl.ds(i * block, block)] = tile[:, block:].astype(BF)


def spread_bias(line, gaps, heads):
    return pl.pallas_call(
        bias_kernel,
        grid_spec=pltpu.PrefetchScalarGridSpec(
            num_scalar_prefetch=1,
            grid=(heads,),
            in_specs=[pl.BlockSpec((8, 2048), lambda h, s: (0, 0))],
            out_specs=pl.BlockSpec((1, 1024, 512), lambda h, s: (h, 0, 0)),
        ),
        out_shape=jax.ShapeDtypeStruct((heads, 1024, 512), BF),
    )(gaps * 256 + 768, line)


def inverse_rms(value):
    return lax.rsqrt(jnp.mean(value * value, -1, keepdims=True) + EPS)


def norm_back(value, inverse, gain, grad):
    scaled = grad * gain
    return inverse * (scaled - value * (inverse * inverse) * jnp.mean(scaled * value, -1, keepdims=True))


def gelu_product(gate_value, up_value):
    return jax.nn.gelu(gate_value, approximate=True) * up_value


def turned(received):
    half = received.shape[0] // 2
    return jnp.concatenate([received[half:], received[:half]], 0).astype(F32)


def gather_rows(local):
    return lax.all_gather(local, "fsdp", axis=0, tiled=True)


def scatter_rows(whole):
    return lax.psum_scatter(whole, "fsdp", scatter_dimension=0, tiled=True)


def per_device(
    decoder_input,
    memory,
    memory_lengths,
    distance_bucket,
    cotangent,
    self_gain,
    self_query,
    self_key,
    self_value,
    self_output,
    bucket_bias,
    cross_gain,
    cross_query,
    cross_key,
    cross_value,
    cross_output,
    feed_gain,
    gate_weight,
    up_weight,
    down_weight,
):
    shards = lax.axis_size("fsdp")
    rep = lax.axis_index("rep")
    side, core = rep // 2, rep % 2
    first = core == 0
    rows = decoder_input.shape[1]
    width = decoder_input.shape[2]
    slots = memory.shape[1]
    half = width // 2
    heads = half // HEAD
    shard_rows = self_query.shape[0]
    hidden_all = gate_weight.shape[1]
    hidden_rows = down_weight.shape[0]
    hidden_half = hidden_rows // 2

    def own_columns(weight):
        return lax.dynamic_slice_in_dim(weight, core * half, half, 1).astype(BF)

    def own_hidden(weight):
        parts = weight.reshape(shard_rows, shards, 2, hidden_half)
        own = lax.dynamic_index_in_dim(parts, core, 2, keepdims=False)
        return own.reshape(shard_rows, hidden_all // 2).astype(BF)

    x_own = decoder_input[0]
    x_pair = jnp.concatenate([x_own, far_swap(x_own)], 0)
    x_all = jnp.concatenate([x_pair, core_swap(x_pair)], 0)
    m_own = memory[0]
    m_pair = jnp.concatenate([m_own, far_swap(m_own)], 0)
    m_all = jnp.concatenate([m_pair, core_swap(m_pair)], 0)
    cot_own = cotangent[0]
    cot = jnp.concatenate([cot_own, core_swap(cot_own)], 0)
    places = jnp.stack([rep, 2 * (1 - side) + core, 2 * side + 1 - core, 2 * (1 - side) + 1 - core])

    columns = jnp.stack(
        [self_gain, cross_gain, feed_gain, jnp.pad(bucket_bias, (0, shard_rows - bucket_bias.shape[0]))], 1
    ).astype(BF)
    pack_one = gather_rows(
        jnp.concatenate(
            [own_columns(self_query), own_columns(self_key), own_columns(self_value), jnp.pad(columns, ((0, 0), (0, 124)))], 1
        )
    )
    pack_two = gather_rows(
        jnp.concatenate(
            [
                own_columns(self_output),
                own_columns(cross_query),
                own_columns(cross_key),
                own_columns(cross_value),
                own_columns(cross_output),
            ],
            1,
        )
    )
    pack_three = gather_rows(jnp.concatenate([own_hidden(gate_weight), own_hidden(up_weight)], 1))
    down_half = lax.dynamic_slice_in_dim(down_weight, core * hidden_half, hidden_half, 0).astype(BF)
    down_matrix = gather_rows(down_half)

    query_one = pack_one[:, :half]
    kv_one = pack_one[:, half : 3 * half]
    gains = pack_one[:, 3 * half : 3 * half + 4].astype(F32)
    gain_one, gain_two, gain_three = gains[:, 0][None], gains[:, 1][None], gains[:, 2][None]
    table = gains[:, 3].reshape(shards, shard_rows)[:, : shard_rows // 2].reshape(2, heads, BUCKETS)
    table = lax.dynamic_index_in_dim(table, core, 0, keepdims=False)
    query_two = pack_two[:, half : 2 * half]
    kv_two = pack_two[:, 2 * half : 4 * half]
    outs = jnp.stack([pack_two[:, :half], pack_two[:, 4 * half :]])
    mine = lax.dynamic_slice_in_dim(outs, core * half, half, 1)
    other = core_swap(lax.dynamic_slice_in_dim(outs, (1 - core) * half, half, 1))
    outs = jnp.concatenate([jnp.where(first, mine, other), jnp.where(first, other, mine)], 2)
    output_one, output_two = outs[0], outs[1]
    gate_matrix = pack_three[:, : hidden_all // 2]
    up_matrix = pack_three[:, hidden_all // 2 :]

    slot = (places[:, None] * slots + jnp.arange(slots, dtype=jnp.int32)[None]).reshape(-1)
    lane = jnp.arange(128, dtype=jnp.int32)[None]
    ones = jnp.where((lane >= 1) & (lane <= 3), 1.0, 0.0)
    extra_two = (jnp.where((lane == 0) & (slot >= memory_lengths[0])[:, None], NEG, 0.0) + ones).astype(BF)
    extra_one = jnp.broadcast_to(ones, (4 * rows, 128)).astype(BF)
    codes = jnp.arange(BUCKETS, dtype=jnp.int32)
    hot = (distance_bucket[None, :] == codes[:, None]).astype(BF)
    line = jnp.einsum("hb,bd->hd", table.astype(BF), hot, preferred_element_type=F32)
    line = jnp.concatenate([jnp.full((heads, 4 * rows), NEG, F32), line], 1)
    line = jnp.pad(line, ((0, 8 - heads), (0, 0)))
    query_places = jnp.stack([places[0], places[2]])
    gaps = (query_places[None, :] - places[:, None]).reshape(-1)
    bias = spread_bias(line, gaps, heads)

    inputs_all = x_all.astype(F32)
    normal_all = inputs_all * inverse_rms(inputs_all)
    n1_all = (normal_all * gain_one).astype(BF)
    n1 = jnp.concatenate([n1_all[:rows], n1_all[2 * rows : 3 * rows]], 0)
    inputs = jnp.concatenate([inputs_all[:rows], inputs_all[2 * rows : 3 * rows]], 0)
    q1 = dot(query_one, n1, TT).astype(BF)
    k1v1 = dot(n1_all, kv_one).astype(BF)
    o1, logs_one = attend(q1, k1v1, extra_one, bias)
    part = dot(o1, output_one, TN)
    middle = inputs + part + turned(core_swap(part.astype(BF)))
    inverse_two = inverse_rms(middle)
    n2 = (middle * inverse_two * gain_two).astype(BF)
    q2 = dot(query_two, n2, TT).astype(BF)
    k2v2 = dot(m_all, kv_two).astype(BF)
    o2, logs_two = attend(q2, k2v2, extra_two)
    part = dot(o2, output_two, TN)
    after = middle + part + turned(core_swap(part.astype(BF)))
    inverse_three = inverse_rms(after)
    n3 = (after * inverse_three * gain_three).astype(BF)
    gate_value = dot(n3, gate_matrix)
    up_value = dot(n3, up_matrix)
    hidden = gelu_product(gate_value, up_value).astype(BF)
    part = dot(hidden, down_matrix)
    output = after[:rows] + part[:rows] + core_swap(part[rows:].astype(BF)).astype(F32)

    cot_low = cot.astype(BF)
    d_hidden = dot(cot_low, down_matrix, NT)
    _, gelu_pull = jax.vjp(gelu_product, gate_value, up_value)
    d_gate, d_up = gelu_pull(d_hidden)
    d_gate, d_up = d_gate.astype(BF), d_up.astype(BF)
    d_down_w = dot(hidden, cot_low, TN).astype(BF)
    d_gate_w = dot(n3, d_gate, TN).astype(BF)
    d_up_w = dot(n3, d_up, TN).astype(BF)
    part = dot(d_gate, gate_matrix, NT) + dot(d_up, up_matrix, NT)
    d_gain_three = jnp.sum(part * (after * inverse_three), 0)
    d_n3 = part + turned(core_swap(part.astype(BF)))
    d_after = cot + norm_back(after, inverse_three, gain_three, d_n3)

    d_after_low = d_after.astype(BF)
    d_output_two = dot(o2, d_after_low).astype(BF)
    d_o2 = dot(output_two, d_after_low, NT).astype(BF)
    d_q2, d_k2, d_v2 = attend_back(q2, k2v2, extra_two, o2, d_o2, logs_two)
    part = dot(d_q2, query_two, TT)
    d_gain_two = jnp.sum(part * (middle * inverse_two), 0)
    d_n2 = part + turned(core_swap(part.astype(BF)))
    d_middle = d_after + norm_back(middle, inverse_two, gain_two, d_n2)
    d_query_two = lax.dot_general(n2, d_q2, TT, preferred_element_type=F32).astype(BF)
    d_key_two = dot(m_all, d_k2, TN).astype(BF)
    d_value_two = dot(m_all, d_v2, TN).astype(BF)
    d_memory = dot(d_k2, kv_two[:, :half], NT) + dot(d_v2, kv_two[:, half:], NT)
    d_memory = d_memory[: 2 * slots] + core_swap(d_memory[2 * slots :].astype(BF)).astype(F32)
    d_memory = d_memory[:slots] + far_swap(d_memory[slots:].astype(BF)).astype(F32)

    d_middle_low = d_middle.astype(BF)
    d_output_one = dot(o1, d_middle_low).astype(BF)
    d_o1 = dot(output_one, d_middle_low, NT).astype(BF)
    d_q1, d_k1, d_v1, d_far = attend_back(q1, k1v1, extra_one, o1, d_o1, logs_one, bias)
    part = dot(d_k1, kv_one[:, :half], NT) + dot(d_v1, kv_one[:, half:], NT)
    part_q = dot(d_q1, query_one, TT)
    none = jnp.zeros((rows, width), F32)
    part = part + jnp.concatenate([part_q[:rows], none, part_q[rows:], none], 0)
    d_gain_one = jnp.sum(part * normal_all, 0)
    d_n1 = part[: 2 * rows] + core_swap(part[2 * rows :].astype(BF)).astype(F32)
    d_n1 = d_n1[:rows] + far_swap(d_n1[rows:].astype(BF)).astype(F32)
    own = inputs_all[:rows]
    d_input = d_middle[:rows] + norm_back(own, inverse_rms(own), gain_one, d_n1)
    d_query_one = lax.dot_general(n1, d_q1, TT, preferred_element_type=F32).astype(BF)
    d_key_one = dot(n1_all, d_k1, TN).astype(BF)
    d_value_one = dot(n1_all, d_v1, TN).astype(BF)
    far = (gaps[:, None] * 256 + jnp.arange(512, dtype=jnp.int32)[None] - 255).reshape(-1)
    below = jnp.sum((distance_bucket[None, :] < codes[:, None]).astype(jnp.int32), 1)
    upto = jnp.sum((distance_bucket[None, :] <= codes[:, None]).astype(jnp.int32), 1)
    inside = ((far[None] >= below[:, None]) & (far[None] < upto[:, None])).astype(F32)
    d_table = jnp.einsum("hd,bd->hb", d_far.reshape(heads, -1), inside, precision=lax.Precision.HIGHEST)

    d_outs = jnp.stack([d_output_one, d_output_two])
    mine = lax.dynamic_slice_in_dim(d_outs, core * half, half, 2)
    other = core_swap(lax.dynamic_slice_in_dim(d_outs, (1 - core) * half, half, 2))
    d_outs = jnp.concatenate([jnp.where(first, mine, other), jnp.where(first, other, mine)], 1)

    def owners(value):
        value = scatter_rows(value)
        value = (value.astype(F32) + far_swap(value).astype(F32)).astype(BF)
        return value, core_swap(value)

    def whole(own, other, axis):
        both = [jnp.where(first, own, other), jnp.where(first, other, own)]
        return jnp.concatenate(both, axis).astype(F32)

    def whole_hidden(own, other):
        both = [jnp.where(first, own, other), jnp.where(first, other, own)]
        both = [b.reshape(shard_rows, shards, 1, hidden_half) for b in both]
        return jnp.concatenate(both, 2).reshape(shard_rows, hidden_all).astype(F32)

    down_own, down_other = owners(d_down_w)
    gu_own, gu_other = owners(jnp.concatenate([d_gate_w, d_up_w], 1))
    cross_own, cross_other = owners(jnp.concatenate([d_query_two, d_key_two, d_value_two, d_outs[1]], 1))
    self_own, self_other = owners(jnp.concatenate([d_query_one, d_key_one, d_value_one, d_outs[0]], 1))
    d_self = [whole(self_own[:, i * half : (i + 1) * half], self_other[:, i * half : (i + 1) * half], 1) for i in range(4)]
    d_cross = [whole(cross_own[:, i * half : (i + 1) * half], cross_other[:, i * half : (i + 1) * half], 1) for i in range(4)]
    wide = hidden_all // 2
    d_gate_out = whole_hidden(gu_own[:, :wide], gu_other[:, :wide])
    d_up_out = whole_hidden(gu_own[:, wide:], gu_other[:, wide:])
    d_down_out = whole(down_own, down_other, 0)

    d_table = d_table.reshape(1, -1)
    d_table = jnp.concatenate([jnp.where(first, d_table, 0.0), jnp.where(first, 0.0, d_table)], 1)[0]
    small = lax.psum(jnp.concatenate([d_gain_one, d_gain_two, d_gain_three, d_table]), ("rep", "fsdp"))
    shard = lax.axis_index("fsdp")
    d_gains = [lax.dynamic_slice_in_dim(small, i * width + shard * shard_rows, shard_rows) for i in range(3)]
    d_bucket = lax.dynamic_slice_in_dim(small, 3 * width + shard * (shard_rows // 2), shard_rows // 2)

    return (
        output[None],
        d_input[None],
        d_memory[None],
        d_gains[0],
        d_self[0],
        d_self[1],
        d_self[2],
        d_self[3],
        d_bucket,
        d_gains[1],
        d_cross[0],
        d_cross[1],
        d_cross[2],
        d_cross[3],
        d_gains[2],
        d_gate_out,
        d_up_out,
        d_down_out,
    )


def solution(mesh):
    split = P("fsdp", "rep", None)
    vector, matrix = P("fsdp"), P("fsdp", None)
    weights = (
        (vector,)
        + (matrix,) * 4
        + (vector, vector)
        + (matrix,) * 4
        + (vector,)
        + (matrix,) * 3
    )
    return jax.shard_map(
        per_device,
        mesh=mesh,
        in_specs=(split, split, vector, P(), split) + weights,
        out_specs=(split, split, split) + weights,
        check_vma=False,
    )
```

time: 1800 us -> 561 us (0.31)
  waiting for transfers between devices: 978 us -> 226 us
  matrix products: 292 us -> 74.5 us
  blocking collectives: 201 us -> 42.2 us
  local copies, waits for them, and re-layouts: 167 us -> 58.3 us
  other arithmetic: 126 us -> 46.3 us
  Pallas kernels: 0 us -> 73.5 us
    reduce_scatter x9 -> x2, waiting for transfers between devices: 364 us -> 0.04 us  [scatter_rows(): return lax.psum_scatter(whole, 'fsdp', scatter_dimension=0, tiled=True)]
    all_gather x15 -> x4, waiting for transfers between devices: 410 us -> 95.6 us  [gather_rows(): return lax.all_gather(local, 'fsdp', axis=0, tiled=True)]
    dot_general x47 -> x33, matrix products: 292 us -> 74.5 us  [the longest x29 71.7 us: dot(): return lax.dot_general(left, right, dims, preferred_element_type=F32)]
    all_to_all x3 -> x0, blocking collectives: 136 us -> none  [the longest x1 56.4 us: per_device(): lax.all_to_all(parted_values, 'rep', split_axis=1, concat_axis=1, tiled=T...]
    convert_element_type x44 -> x23, other arithmetic: 84.9 us -> 7.71 us  [the longest x1 2.34 us: per_device(): (jnp.where((lane == 0) & (slot >= memory_lengths[0])[:, None], NEG, 0.0)...]
    pallas_call x0 -> x5, Pallas kernels: none -> 73.5 us  [the longest x2 43.2 us: attend_back(): pl.pallas_call(functools.partial(attend_back_kernel, chunk, bias is not N...]
    unnamed x29 -> x10, waiting for transfers between devices: 141 us -> 69.6 us
    ppermute x0 -> x24, waiting for transfers between devices: none -> 60.6 us  [the longest x8 58.3 us: far_swap(): return lax.ppermute(value, 'rep', FAR)]
  transfers between devices with their start and end apart: 28 -> 32, of which waited for: 19 -> 11; matrix products, arithmetic and copies ran while one was open for 25% -> 26% of each run, Pallas kernels for 0% -> 13%
where the time goes in v1:
time: 561 us; the launch traced here: 552 us
  waiting for transfers between devices  226 us (40%)
  matrix products  74.5 us (13%)
  Pallas kernels  73.5 us (13%)
  local copies, waits for them, and re-layouts  58.3 us (10%)
  other arithmetic  46.3 us (8%)
  blocking collectives  42.2 us (8%)
  between operations  16.2 us (3%)
  starting transfers between devices  15.2 us (3%)
    all_gather x4, waiting for transfers between devices, gather_rows(): return lax.all_gather(local, 'fsdp', axis=0, tiled=True)  95.6 us
    dot_general x29, matrix products, dot(): return lax.dot_general(left, right, dims, preferred_element_type=F32)  71.7 us
    unnamed x10, waiting for transfers between devices  69.6 us
    ppermute x8, waiting for transfers between devices, far_swap(): return lax.ppermute(value, 'rep', FAR)  58.3 us
    pallas_call x2, Pallas kernels, attend_back(): pl.pallas_call(functools.partial(attend_back_kernel, chunk, bias is not N...  43.2 us
    psum x1, blocking collectives, per_device(): lax.psum(jnp.concatenate([d_gain_one, d_gain_two, d_gain_three, d_table])...  42.2 us
    unnamed x153, local copies, waits for them, and re-layouts  37.3 us
    pallas_call x2, Pallas kernels, attend(): pl.pallas_call(functools.partial(attend_kernel, chunk, bias is not None),...  24.4 us
  transfers between devices with their start and end apart: 32, of which 11 were waited for; matrix products, arithmetic and copies ran while one was open for 26% of the time, Pallas kernels for 13%

profile of v1, /device:TPU:0, one launch (start us, length us, event | category | flops | bytes accessed | tf_op | source)
XLA Modules:
  0.0 552.0 jit_solution(8217220117599854296)
XLA Ops:
  21.0 3.0 collective-permute-start
  25.7 8.2 %collective-permute-done = bf16[256,768]{1,0:T(8,128)(2,1)S(1)} collective-permute-done((bf16[256,768]{1,0:T(8,128)(2,1)S(1)}, bf16[256,768]{1,0:T(8,128)(2,1)S(1)}, u32[]{:S(2)}, u32[]{:S(2)}) %collective-permute-start) | collective-permute-done | bytes 393248 | tf_op jit(solution)/shard_map/ppermute | solution.py:30
  40.0 18.5 %collective-permute-done.4 = bf16[768,768]{1,0:T(8,128)(2,1)} collective-permute-done((bf16[768,768]{1,0:T(8,128)(2,1)}, bf16[768,768]{1,0:T(8,128)(2,1)}, u32[]{:S(2)}, u32[]{:S(2)}) %collective-permute-start.4) | collective-permute-done | bytes 1179680 | tf_op jit(solution)/shard_map/ppermute | solution.py:30
  58.5 2.8 pad_maximum_fusion.2
  66.5 2.6 convolution_convert_fusion.16.refs_0_
  69.2 53.7 %all-gather.7.cloned.1.call-done = bf16[768,1920]{1,0:T(8,128)(2,1)} async-done(((bf16[96,1920]{1,0:T(8,128)(2,1)}), bf16[768,1920]{1,0:T(8,128)(2,1)}) %all-gather.7.cloned.1.call-update) | async-done | bytes 2949136 | tf_op jit(solution)/shard_map/all_gather | solution.py:271
  125.5 5.9 %shard_map.331.refs_4_.refs_7_ = bf16[6,1024,512]{2,1,0:T(8,128)(2,1)} custom-call(s32[8]{0:T(128)} %broadcast_add_fusion.starts, f32[8,2048]{1,0:T(8,128)} %pad_select_fusion.line), custom_call_target="tpu_custom_call" | custom-call | tf_op jit(solution)/shard_map/pallas_call | solution.py:240
  131.4 4.4 convolution_convert_fusion.4.refs_1_.refs_2_
  136.5 8.1 %shard_map.332 = (bf16[384,512]{1,0:T(8,128)(2,1)}, f32[3,8,512]{2,1,0:T(8,128)}) custom-call(bf16[384,512]{1,0:T(8,128)(2,1)} %convolution_convert_fusion.16.refs_0_, bf16[1024,768]{1,0:T(8,128)(2,1)} %convolution_convert_fusion.4.refs_1_.refs_2_, bf16[1024,768]{1,0:T(8,128)(2,1)} %convolution_convert_fusion.4.refs_1_.refs_2_, ...), custom_call_target="tpu_custom_call" | custom-call | flops 1610612736 | bytes 1572864 | tf_op jit(solution)/shard_map/pallas_call | solution.py:116
  148.0 8.0 %convolution_convert_fusion.refs_1_.refs_2_ = bf16[3072,768]{1,0:T(8,128)(2,1)} fusion(bf16[768,1920]{1,0:T(8,128)(2,1)S(1)} %copy-done.21, bf16[1536,768]{1,0:T(8,128)(2,1)} %collective-permute-done.5, bf16[768,768]{1,0:T(8,128)(2,1)} %collective-permute-done.4, bf16[768,768]{1,0:T(8,128)(2,1)S(1)} %bitcast.137), kind=kOutput, calls=%fused_computation.1 | convolution fusion | flops 3640393728 | bytes 10616832 | tf_op jit(solution)/shard_map/dot_general | solution.py:34
  159.1 16.2 %shard_map.333 = (bf16[384,512]{1,0:T(8,128)(2,1)}, f32[3,8,512]{2,1,0:T(8,128)}) custom-call(bf16[384,512]{1,0:T(8,128)(2,1)} %convolution_convert_fusion.15.refs_0_, bf16[3072,768]{1,0:T(8,128)(2,1)} %convolution_convert_fusion.refs_1_.refs_2_, bf16[3072,768]{1,0:T(8,128)(2,1)} %convolution_convert_fusion.refs_1_.refs_2_, ...), custom_call_target="tpu_custom_call" | custom-call | flops 4831838208 | bytes 4718592 | tf_op jit(solution)/shard_map/pallas_call | solution.py:116
  184.1 4.1 fusion.14
  190.6 39.0 %all-gather.11.cloned.1.call-done = bf16[1024,768]{1,0:T(8,128)(2,1)} async-done(((bf16[128,768]{1,0:T(8,128)(2,1)}), bf16[1024,768]{1,0:T(8,128)(2,1)}) %all-gather.11.cloned.1.call-update) | async-done | bytes 1572880 | tf_op jit(solution)/shard_map/all_gather | solution.py:271
  229.6 6.9 %multiply_convert_fusion.1 = (bf16[512,1024]{1,0:T(8,128)(2,1)}, bf16[512,1024]{1,0:T(8,128)(2,1)}, bf16[512,1024]{1,0:T(8,128)(2,1)S(1)}) fusion(f32[512,1024]{1,0:T(8,128)} %fusion.14, f32[512,1024]{1,0:T(8,128)} %fusion.10, bf16[1024,768]{1,0:T(8,128)(2,1)} %all-gather.11.cloned.1.call-done, f32[256,768]{1,0:T(8,128)} %collective-permute-done.8, ...), kind=kOutput, calls=%fused_computation.25 | convolution fusion | flops 820510720 | bytes 10485760 | tf_op jit(solution)/shard_map/dot_general | solution.py:34
  237.4 3.6 convolution_convert_fusion.1
  241.1 2.9 fusion.12
  244.1 2.4 fusion.102
  257.7 28.3 %shard_map.334 = (bf16[384,512]{1,0:T(8,128)(2,1)}, bf16[3072,384]{1,0:T(8,128)(2,1)}, bf16[3072,384]{1,0:T(8,128)(2,1)}) custom-call(bf16[384,512]{1,0:T(8,128)(2,1)} %convolution_convert_fusion.15.refs_0_, bf16[3072,768]{1,0:T(8,128)(2,1)} %convolution_convert_fusion.refs_1_.refs_2_, bf16[3072,768]{1,0:T(8,128)(2,1)} %convolution_convert_fusion.refs_1_.refs_2_, ...), custom_call_target="tpu_custom_call" | custom-call | flops 12079595520 | bytes 9437184 | tf_op jit(solution)/shard_map/pallas_call | solution.py:213
  295.9 14.9 %shard_map.335 = (bf16[384,512]{1,0:T(8,128)(2,1)}, bf16[1024,384]{1,0:T(8,128)(2,1)}, bf16[1024,384]{1,0:T(8,128)(2,1)}, f32[3,2,8,512]{3,2,1,0:T(8,128)}) custom-call(bf16[384,512]{1,0:T(8,128)(2,1)} %convolution_convert_fusion.16.refs_0_, bf16[1024,768]{1,0:T(8,128)(2,1)} %convolution_convert_fusion.4.refs_1_.refs_2_, ...), custom_call_target="tpu_custom_call" | custom-call | flops 4026531840 | bytes 3145728 | tf_op jit(solution)/shard_map/pallas_call | solution.py:213
  318.6 4.4 copy.112
  323.4 4.6 fusion.35
  328.0 3.7 convolution_add_fusion
  335.6 4.9 convolution_convert_fusion.11
  340.5 4.3 convolution_convert_fusion.12
  351.6 2.5 copy.114
  361.8 42.2 %psum.7 = f32[2688]{0:T(1024)S(1)} all-reduce(f32[2688]{0:T(1024)S(1)} %pad_maximum_fusion.16), channel_id=1, replica_groups=mesh['rep'=4,'fsdp'=8] {'rep','fsdp'}, use_global_device_ids=true, to_apply=%region_12.13 | all-reduce | flops 2688 | bytes 21504 | tf_op jit(solution)/shard_map/psum | solution.py:493
  409.0 3.6 slice_add_fusion
  417.2 2.7 fusion.22
  421.0 28.0 %collective-permute-done.20 = bf16[96,2048]{1,0:T(8,128)(2,1)S(1)} collective-permute-done((bf16[96,2048]{1,0:T(8,128)(2,1)}, bf16[96,2048]{1,0:T(8,128)(2,1)S(1)}, u32[]{:S(2)}, u32[]{:S(2)}) %collective-permute-start.20) | collective-permute-done | bytes 393248 | tf_op jit(solution)/shard_map/ppermute | solution.py:30
  451.1 3.0 fusion
  457.1 69.2 %reduce-scatter.15.cloned.1.call-done = bf16[96,1536]{1,0:T(8,128)(2,1)} async-done(((bf16[768,1536]{1,0:T(8,128)(2,1)}), bf16[96,1536]{1,0:T(8,128)(2,1)}) %reduce-scatter.15.cloned.1.call-update) | async-done | bytes 294928
  533.8 3.6 collective-permute-done.18
  (343 shorter events, 125.6 us)
Async XLA Ops:
  7.2 55.4 %all-gather.5.cloned.1.call-start = ((), (), s32[]{:S(2)}) async-start(), calls=%async_computation.4 | async-start | bytes 2211840 | tf_op jit(solution)/shard_map/all_gather | solution.py:271
  12.2 110.6 %all-gather.7.cloned.1.call-start = ((), (), s32[]{:S(2)}) async-start(), calls=%async_computation.5 | async-start | bytes 3317760 | tf_op jit(solution)/shard_map/all_gather | solution.py:271
  17.8 166.4 %all-gather.9.cloned.1.call-start = ((), (), s32[]{:S(2)}) async-start(), calls=%async_computation.6 | async-start | bytes 3538944 | tf_op jit(solution)/shard_map/all_gather | solution.py:271
  21.0 208.6 %all-gather.11.cloned.1.call-start = ((), (), s32[]{:S(2)}) async-start(), calls=%async_computation.7 | async-start | bytes 1769472 | tf_op jit(solution)/shard_map/all_gather | solution.py:271
  21.0 12.9 %collective-permute-start = (bf16[256,768]{1,0:T(8,128)(2,1)S(1)}, bf16[256,768]{1,0:T(8,128)(2,1)S(1)}, u32[]{:S(2)}, u32[]{:S(2)}) collective-permute-start(bf16[256,768]{1,0:T(8,128)(2,1)S(1)} %bitcast.123), channel_id=1, source_target_pairs={{0,16},{16,0},{8,24},{24,8},{1,17},{17,1},{9,25},{25,9},{2,18},{18... | collective-permute-start | bytes 1179656 | tf_op jit(solution)/shard_map/ppermute | solution.py:30
  24.0 34.5 %collective-permute-start.4 = (bf16[768,768]{1,0:T(8,128)(2,1)}, bf16[768,768]{1,0:T(8,128)(2,1)}, u32[]{:S(2)}, u32[]{:S(2)}) collective-permute-start(bf16[768,768]{1,0:T(8,128)(2,1)} %bitcast.135), channel_id=1, source_target_pairs={{0,16},{16,0},{8,24},{24,8},{1,17},{17,1},{9,25},{25,9},{2,18},{18... | collective-permute-start | bytes 3538952 | tf_op jit(solution)/shard_map/ppermute | solution.py:30
  24.8 381.8 %reduce-scatter.11.cloned.1.call-start = ((), (), s32[]{:S(2)}) async-start(), calls=%async_computation.9 | async-start | bytes 1769472 | tf_op jit(solution)/shard_map/reduce_scatter | solution.py:275
  34.0 3.2 collective-permute-start.1
  61.4 86.0 %collective-permute-start.5 = (bf16[1536,768]{1,0:T(8,128)(2,1)}, bf16[1536,768]{1,0:T(8,128)(2,1)}, u32[]{:S(2)}, u32[]{:S(2)}) collective-permute-start(bf16[1536,768]{1,0:T(8,128)(2,1)} %pad_maximum_fusion.2), channel_id=1, source_target_pairs={{0,8},{8,0},{16,24},{24,16},{1,9},{9,1},{17,25},{25,17},{2,10},{10... | collective-permute-start | bytes 7077896 | tf_op jit(solution)/shard_map/ppermute | solution.py:26
  124.8 19.9 %collective-permute-start.2 = (bf16[2,384,384]{1,2,0:T(8,128)(2,1)S(1)}, bf16[2,384,384]{1,2,0:T(8,128)(2,1)}, u32[]{:S(2)}, u32[]{:S(2)}) collective-permute-start(bf16[2,384,384]{1,2,0:T(8,128)(2,1)S(1)} %fusion.31), channel_id=1, source_target_pairs={{0,8},{8,0},{16,24},{24,16},{1,9},{9,1},{17,25},{25,17},{2,10},{10... | collective-permute-start | bytes 1769480 | tf_op jit(solution)/shard_map/ppermute | solution.py:26
  146.7 9.2 %collective-permute-start.3 = (bf16[512,768]{1,0:T(8,128)(2,1)S(1)}, bf16[512,768]{1,0:T(8,128)(2,1)S(1)}, u32[]{:S(2)}, u32[]{:S(2)}) collective-permute-start(bf16[512,768]{1,0:T(8,128)(2,1)S(1)} %get-tuple-element.188), channel_id=1, source_target_pairs={{0,8},{8,0},{16,24},{24,16},{1,9},{9,1},{17,25},{25,17},{2,10},{10... | collective-permute-start | bytes 2359304 | tf_op jit(solution)/shard_map/ppermute | solution.py:26
  176.9 2.8 collective-permute-start.6
  177.5 13.1 %collective-permute-start.8 = (f32[256,768]{1,0:T(8,128)}, f32[256,768]{1,0:T(8,128)}, u32[]{:S(2)}, u32[]{:S(2)}) collective-permute-start(f32[256,768]{1,0:T(8,128)} %bitcast.17), channel_id=1, source_target_pairs={{0,8},{8,0},{16,24},{24,16},{1,9},{9,1},{17,25},{25,17},{2,10},{10... | collective-permute-start | bytes 2359304 | tf_op jit(solution)/shard_map/ppermute | solution.py:26
  241.0 174.8 %reduce-scatter.9.cloned.1.call-start = ((), (), s32[]{:S(2)}) async-start(), calls=%async_computation.8 | async-start | bytes 3538944 | tf_op jit(solution)/shard_map/reduce_scatter | solution.py:275
  246.5 4.3 collective-permute-start.9
  250.8 203.6 %reduce-scatter.13.cloned.1.call-start = ((), (), s32[]{:S(2)}) async-start(), calls=%async_computation.10 | async-start | bytes 2654208
  288.0 3.1 collective-permute-start.10
  290.3 64.0 %collective-permute-start.7 = (bf16[256,768]{1,0:T(8,128)(2,1)}, bf16[256,768]{1,0:T(8,128)(2,1)}, u32[]{:S(2)}, u32[]{:S(2)}) collective-permute-start(bf16[256,768]{1,0:T(8,128)(2,1)} %slice.475), channel_id=1, source_target_pairs={{0,8},{8,0},{16,24},{24,16},{1,9},{9,1},{17,25},{25,17},{2,10},{10... | collective-permute-start | bytes 1179656 | tf_op jit(solution)/shard_map/ppermute | solution.py:26
  294.3 20.3 %collective-permute-start.15 = (bf16[2,384,384]{1,2,0:T(8,128)(2,1)}, bf16[2,384,384]{1,2,0:T(8,128)(2,1)}, u32[]{:S(2)}, u32[]{:S(2)}) collective-permute-start(bf16[2,384,384]{1,2,0:T(8,128)(2,1)} %fusion.29), channel_id=1, source_target_pairs={{0,8},{8,0},{16,24},{24,16},{1,9},{9,1},{17,25},{25,17},{2,10},{10... | collective-permute-start | bytes 1769480 | tf_op jit(solution)/shard_map/ppermute | solution.py:26
  323.0 203.3 %reduce-scatter.15.cloned.1.call-start = ((), (), s32[]{:S(2)}) async-start(), calls=%async_computation.11 | async-start | bytes 2654208
  333.4 75.6 %collective-permute-start.13 = (bf16[1536,768]{1,0:T(8,128)(2,1)}, bf16[1536,768]{1,0:T(8,128)(2,1)}, u32[]{:S(2)}, u32[]{:S(2)}) collective-permute-start(bf16[1536,768]{1,0:T(8,128)(2,1)} %slice.471), channel_id=1, source_target_pairs={{0,8},{8,0},{16,24},{24,16},{1,9},{9,1},{17,25},{25,17},{2,10},{10... | collective-permute-start | bytes 7077896 | tf_op jit(solution)/shard_map/ppermute | solution.py:26
  350.5 7.3 %collective-permute-start.11 = (bf16[512,768]{1,0:T(8,128)(2,1)}, bf16[512,768]{1,0:T(8,128)(2,1)}, u32[]{:S(2)}, u32[]{:S(2)}) collective-permute-start(bf16[512,768]{1,0:T(8,128)(2,1)} %slice.473), channel_id=1, source_target_pairs={{0,8},{8,0},{16,24},{24,16},{1,9},{9,1},{17,25},{25,17},{2,10},{10... | collective-permute-start | bytes 2359304 | tf_op jit(solution)/shard_map/ppermute | solution.py:26
  359.6 45.6 %collective-permute-start.12 = (bf16[256,768]{1,0:T(8,128)(2,1)S(1)}, bf16[256,768]{1,0:T(8,128)(2,1)S(1)}, u32[]{:S(2)}, u32[]{:S(2)}) collective-permute-start(bf16[256,768]{1,0:T(8,128)(2,1)S(1)} %slice.474), channel_id=1, source_target_pairs={{0,16},{16,0},{8,24},{24,8},{1,17},{17,1},{9,25},{25,9},{2,18},{18... | collective-permute-start | bytes 1179656 | tf_op jit(solution)/shard_map/ppermute | solution.py:30
  406.6 8.4 %collective-permute-start.22 = (bf16[128,768]{1,0:T(8,128)(2,1)}, bf16[128,768]{1,0:T(8,128)(2,1)S(1)}, u32[]{:S(2)}, u32[]{:S(2)}) collective-permute-start(bf16[128,768]{1,0:T(8,128)(2,1)} %reduce-scatter.11.cloned.1.call-done), channel_id=1, source_target_pairs={{0,16},{16,0},{8,24},{24,8},{1,17},{17,1},{9,25},{25,9},{2,18},{18... | collective-permute-start | bytes 589832 | tf_op jit(solution)/shard_map/ppermute | solution.py:30
  414.9 36.2 %collective-permute-start.14 = (bf16[768,768]{1,0:T(8,128)(2,1)S(1)}, bf16[768,768]{1,0:T(8,128)(2,1)}, u32[]{:S(2)}, u32[]{:S(2)}) collective-permute-start(bf16[768,768]{1,0:T(8,128)(2,1)S(1)} %slice.472), channel_id=1, source_target_pairs={{0,16},{16,0},{8,24},{24,8},{1,17},{17,1},{9,25},{25,9},{2,18},{18... | collective-permute-start | bytes 3538952 | tf_op jit(solution)/shard_map/ppermute | solution.py:30
  415.8 4.2 collective-permute-start.23
  415.9 33.1 %collective-permute-start.20 = (bf16[96,2048]{1,0:T(8,128)(2,1)}, bf16[96,2048]{1,0:T(8,128)(2,1)S(1)}, u32[]{:S(2)}, u32[]{:S(2)}) collective-permute-start(bf16[96,2048]{1,0:T(8,128)(2,1)} %reduce-scatter.9.cloned.1.call-done), channel_id=1, source_target_pairs={{0,16},{16,0},{8,24},{24,8},{1,17},{17,1},{9,25},{25,9},{2,18},{18... | collective-permute-start | bytes 1179656 | tf_op jit(solution)/shard_map/ppermute | solution.py:30
  450.1 79.0 %collective-permute-start.21 = (bf16[96,2048]{1,0:T(8,128)(2,1)S(1)}, bf16[96,2048]{1,0:T(8,128)(2,1)S(1)}, u32[]{:S(2)}, u32[]{:S(2)}) collective-permute-start(bf16[96,2048]{1,0:T(8,128)(2,1)S(1)} %add_convert_fusion.1), channel_id=1, source_target_pairs={{0,8},{8,0},{16,24},{24,16},{1,9},{9,1},{17,25},{25,17},{2,10},{10... | collective-permute-start | bytes 1179656 | tf_op jit(solution)/shard_map/ppermute | solution.py:26
  455.5 78.1 %collective-permute-start.16 = (bf16[96,1536]{0,1:T(8,128)(2,1)S(1)}, bf16[96,1536]{0,1:T(8,128)(2,1)S(1)}, u32[]{:S(2)}, u32[]{:S(2)}) collective-permute-start(bf16[96,1536]{0,1:T(8,128)(2,1)S(1)} %copy.113), channel_id=1, source_target_pairs={{0,16},{16,0},{8,24},{24,8},{1,17},{17,1},{9,25},{25,9},{2,18},{18... | collective-permute-start | bytes 884744 | tf_op jit(solution)/shard_map/ppermute | solution.py:30
  527.5 9.9 %collective-permute-start.18 = (bf16[96,1536]{0,1:T(8,128)(2,1)S(1)}, bf16[96,1536]{0,1:T(8,128)(2,1)S(1)}, u32[]{:S(2)}, u32[]{:S(2)}) collective-permute-start(bf16[96,1536]{0,1:T(8,128)(2,1)S(1)} %copy.115), channel_id=1, source_target_pairs={{0,16},{16,0},{8,24},{24,8},{1,17},{17,1},{9,25},{25,9},{2,18},{18... | collective-permute-start | bytes 884744 | tf_op jit(solution)/shard_map/ppermute | solution.py:30
  533.7 3.9 collective-permute-start.17
  537.5 3.8 collective-permute-start.19
  (63 other events, 343.4 us)
Sparse Core Ops, SparseCore 0:
  12.3 50.2 all-gather.4
  65.3 57.4 all-gather.6
  125.0 59.0 all-gather.8
  186.7 42.7 all-gather.10
  241.2 63.6 reduce-scatter.10
  308.7 73.5 reduce-scatter.8
  386.1 68.1 reduce-scatter.12
  458.2 68.0 reduce-scatter.14
